TPU v7x, 32 devices: a whole 2x2x4 slice. The times are simulated.
32 devices in a mesh: judge: 4 (over y, core), fsdp: 8 (over z, x).
Axes of the slice: x: 2, y: 2, z: 4, core: 2. Of those that a mesh axis runs over, the one named last changes fastest.
Arguments:
- hidden: bfloat16 [4, 8192, 4096], P('judge', 'fsdp'), may hold values from -32 to 32
- lengths: int32 [16], replicated, may hold values from 128 to 512
- duplicate_group_index: int32 [16], replicated, may hold values from 0 to 3, as said below
- attn_gain: bfloat16 [4, 4096], P('judge', 'fsdp'), may hold values from 0.5 to 1.5
- w_query: bfloat16 [4, 4096, 4096], P('judge', None, 'fsdp'), may hold values from -1 to 1
- w_key: bfloat16 [4, 4096, 1024], P('judge', 'fsdp'), may hold values from -1 to 1
- w_value: bfloat16 [4, 4096, 1024], P('judge', 'fsdp'), may hold values from -0.09375 to 0.09375
- w_out: bfloat16 [4, 4096, 4096], P('judge', 'fsdp'), may hold values from -0.09375 to 0.09375
- mlp_gain: bfloat16 [4, 4096], P('judge', 'fsdp'), may hold values from 0.5 to 1.5
- w_gate: bfloat16 [4, 4096, 14336], P('judge', None, 'fsdp'), may hold values from -0.09375 to 0.09375
- w_up: bfloat16 [4, 4096, 14336], P('judge', None, 'fsdp'), may hold values from -0.09375 to 0.09375
- w_down: bfloat16 [4, 14336, 4096], P('judge', 'fsdp'), may hold values from -0.046875 to 0.046875
- final_gain: bfloat16 [4, 4096], P('judge', 'fsdp'), may hold values from 0.5 to 1.5
- reward_head: float32 [4, 4096], P('judge'), may hold values from -8 to 8
Outputs:
- survivor_weights: float32 [16], replicated
- cluster_features: float32 [4, 4096], P(None, 'fsdp')
Inputs may be any that keep to these rules, and one draw needn't show every extreme that they name: `duplicate_group_index`: every cluster holds exactly four candidates.
All inputs are finite; a program needn't handle non-finite values.
Results may differ from a plain program's by a relative error of at most 0.003.
Values may be sent and summed in bfloat16 or wider, within the bound.
A program may use at most 192 MiB of HBM per device.

v0:
```python
import math

import jax
import jax.numpy as jnp
from jax import lax
from jax.sharding import PartitionSpec as P

KV_HEADS = 8
HEAD_DIM = 128
LEN = 512


EPS = 1e-05
ROPE_BASE = 500000.0


def row_scale(v):
    return lax.rsqrt(jnp.mean(v * v, axis=-1, keepdims=True) + EPS)


def angles(position):
    half = HEAD_DIM // 2
    freq = jnp.exp(jnp.arange(half, dtype=jnp.float32) * (-2.0 * math.log(ROPE_BASE) / HEAD_DIM))
    turned = position[..., None] * freq
    return (jnp.cos(turned), jnp.sin(turned))


def rotate(v, cosine, sine):
    half = HEAD_DIM // 2
    first = v[..., :half]
    second = v[..., half:]
    return jnp.concatenate(
        [first * cosine - second * sine, second * cosine + first * sine], axis=-1
    )


def remaining_candidates(judge_panel, duplicate_group_index, duplicate_groups):
    same = duplicate_group_index[:, None] == duplicate_group_index[None, :]
    top = jnp.max(jnp.where(same, judge_panel[None, :], -1e30), axis=1)
    expo = jnp.exp(judge_panel - top)
    total = jnp.sum(jnp.where(same, expo[None, :], 0.0), axis=1)
    weight_values = expo / total
    panel_member = (
        duplicate_group_index[:, None] == jnp.arange(duplicate_groups, dtype=jnp.int32)[None, :]
    ).astype(jnp.float32)
    return (weight_values, panel_member)


def body(
    hidden,
    lengths,
    duplicate_group_index,
    attn_gain,
    w_query,
    w_key,
    w_value,
    w_out,
    mlp_gain,
    w_gate,
    w_up,
    w_down,
    final_gain,
    reward_head,
):
    reward_judges = lax.axis_size("judge")
    devices = lax.axis_size("fsdp")
    me = lax.axis_index("fsdp")
    tokens = hidden[0]
    tok_dev, width = tokens.shape
    seq_dev = tok_dev // LEN
    cands = lengths.shape[0]
    duplicate_groups = cands // 4
    groups = width // HEAD_DIM // KV_HEADS
    column_count = width // devices
    col_start = me * column_count
    own_len = lax.dynamic_slice_in_dim(lengths, me * seq_dev, seq_dev)
    last_index = jnp.arange(seq_dev, dtype=jnp.int32) * LEN + own_len - 1
    own_last = tokens[last_index]
    x_last, gain_attn, gain_mlp, gain_final = (
        lax.all_gather(own_last, "fsdp", axis=0, tiled=True),
        lax.all_gather(attn_gain[0], "fsdp", axis=0, tiled=True),
        lax.all_gather(mlp_gain[0], "fsdp", axis=0, tiled=True),
        lax.all_gather(final_gain[0], "fsdp", axis=0, tiled=True),
    )
    x_last = x_last.astype(jnp.float32)
    scale = row_scale(tokens.astype(jnp.float32))
    key_rows, value_rows = (
        lax.all_gather(w_key[0], "fsdp", axis=0, tiled=True),
        lax.all_gather(w_value[0], "fsdp", axis=0, tiled=True),
    )
    tok_norm = (tokens.astype(jnp.float32) * scale * gain_attn.astype(jnp.float32)).astype(
        jnp.bfloat16
    )
    keys = jnp.dot(tok_norm, key_rows, preferred_element_type=jnp.float32)
    values = jnp.dot(tok_norm, value_rows, preferred_element_type=jnp.float32)
    key_cos, key_sin = angles(jnp.arange(LEN, dtype=jnp.float32))
    keys = keys.reshape(seq_dev, LEN, KV_HEADS, HEAD_DIM)
    keys = rotate(keys, key_cos[None, :, None, :], key_sin[None, :, None, :]).astype(jnp.bfloat16)
    values = values.astype(jnp.bfloat16).reshape(seq_dev, LEN, KV_HEADS, HEAD_DIM)
    q_norm = (x_last * row_scale(x_last) * gain_attn.astype(jnp.float32)).astype(jnp.bfloat16)
    q_part = jnp.dot(q_norm, w_query[0], preferred_element_type=jnp.float32)
    q_part = q_part.reshape(cands, q_part.shape[1] // HEAD_DIM, HEAD_DIM)
    cosine, sine = angles((lengths - 1).astype(jnp.float32))
    q_part = (
        rotate(q_part, cosine[:, None, :], sine[:, None, :]).astype(jnp.bfloat16).reshape(cands, -1)
    )
    q_own = lax.all_to_all(q_part, "fsdp", split_axis=0, concat_axis=1, tiled=True)
    q_own = q_own.reshape(seq_dev, KV_HEADS, groups, HEAD_DIM)
    scores = jnp.einsum(
        "skgd,slkd->skgl", q_own, keys, preferred_element_type=jnp.float32
    ) * HEAD_DIM ** (-0.5)
    valid = jnp.arange(LEN, dtype=jnp.int32)[None, None, None, :] < own_len[:, None, None, None]
    scores = jnp.where(valid, scores, -1e30)
    top = jnp.max(scores, axis=-1, keepdims=True)
    expo = jnp.exp(scores - top)
    probs = (expo / jnp.sum(expo, axis=-1, keepdims=True)).astype(jnp.bfloat16)
    mixed = jnp.einsum("skgl,slkd->skgd", probs, values, preferred_element_type=jnp.float32)
    mixed = mixed.reshape(seq_dev, width).astype(jnp.bfloat16)
    head_rows = lax.all_to_all(mixed, "fsdp", split_axis=1, concat_axis=0, tiled=True)
    attn = lax.psum(jnp.dot(head_rows, w_out[0], preferred_element_type=jnp.float32), "fsdp")
    after_attn = x_last + attn
    m_norm = (after_attn * row_scale(after_attn) * gain_mlp.astype(jnp.float32)).astype(
        jnp.bfloat16
    )
    gate = jnp.dot(m_norm, w_gate[0], preferred_element_type=jnp.float32)
    up = jnp.dot(m_norm, w_up[0], preferred_element_type=jnp.float32)
    act = (jax.nn.silu(gate) * up).astype(jnp.bfloat16)
    down_terms = jnp.dot(act, w_down[0], preferred_element_type=jnp.float32)
    down = lax.psum(down_terms, "fsdp")
    after_mlp = after_attn + down
    features = after_mlp * row_scale(after_mlp) * gain_final.astype(jnp.float32)
    score = jnp.dot(features, reward_head[0], precision=lax.Precision.HIGHEST)
    feature_cols = lax.dynamic_slice_in_dim(features, col_start, column_count, 1)
    total_cols, score_total = lax.psum((feature_cols, score), "judge")
    weight_values, panel_member = remaining_candidates(
        score_total / reward_judges, duplicate_group_index, duplicate_groups
    )
    cluster_cols = jnp.dot(
        panel_member.T,
        weight_values[:, None] * (total_cols / reward_judges),
        precision=lax.Precision.HIGHEST,
    )
    return (weight_values, cluster_cols)


def solution(mesh):
    in_specs = (
        P("judge", "fsdp", None),
        P(),
        P(),
        P("judge", "fsdp"),
        P("judge", None, "fsdp"),
        P("judge", "fsdp", None),
        P("judge", "fsdp", None),
        P("judge", "fsdp", None),
        P("judge", "fsdp"),
        P("judge", None, "fsdp"),
        P("judge", None, "fsdp"),
        P("judge", "fsdp", None),
        P("judge", "fsdp"),
        P("judge", None),
    )
    out_specs = (P(), P(None, "fsdp"))
    return jax.shard_map(body, mesh=mesh, in_specs=in_specs, out_specs=out_specs, check_vma=False)
```

profile of v0, /device:TPU:0, one launch (start us, length us, event | category | flops | bytes accessed | tf_op | source)
XLA Modules:
  0.0 487.0 jit_solution(11033750207211315531)
XLA Ops:
  7.2 0.7 all-gather.10.cloned.1.call-update
  8.0 0.7 all-gather.12.cloned.1.call-update
  8.7 28.3 %all-gather.1 = bf16[1,4096]{1,0:T(2,128)(2,1)S(1)} all-gather(bf16[1,512]{1,0:T(2,128)(2,1)} %param.17), channel_id=3, replica_groups=mesh['judge'=4,'fsdp'=8] {'fsdp'}, dimensions={1}, use_global_device_ids=true | all-gather | bytes 9216 | tf_op jit(solution)/shard_map/all_gather | solution.py:81
  37.0 0.7 compare_select_fusion.2
  37.7 5.1 %gather_fusion = bf16[2,4096]{1,0:T(2,128)(2,1)S(1)} fusion(bf16[1024,4096]{1,0:T(8,128)(2,1)} %bitcast.70, s32[1024]{0:T(1024)S(1)} %pad_clamp_fusion), kind=kCustom, calls=%fused_computation | custom fusion | bytes 32776 | tf_op jit(solution)/shard_map/gather | solution.py:78
  42.8 31.3 %all-gather.6 = bf16[8,2,4096]{2,1,0:T(2,128)(2,1)S(1)} all-gather(bf16[1,2,4096]{2,1,0:T(2,128)(2,1)S(1)} %bitcast.82), channel_id=2, replica_groups=mesh['judge'=4,'fsdp'=8] {'fsdp'}, dimensions={0}, use_global_device_ids=true | all-gather | bytes 147456 | tf_op jit(solution)/shard_map/all_gather | solution.py:80
  74.1 6.4 %copy.43 = bf16[512,4096]{1,0:T(8,128)(2,1)} copy(bf16[512,4096]{0,1:T(8,128)(2,1)} %bitcast.75) | data formatting | bytes 8388608 | tf_op jit(solution)/shard_map/dot_general | solution.py:101
  80.8 3.4 fusion.47
  84.4 0.6 convert_element_type.75
  85.0 3.9 all-to-all-start
  89.2 5.1 %fusion.1 = f32[1024]{0:T(1024)S(1)} fusion(bf16[1,1024,4096]{2,1,0:T(8,128)(2,1)} %param.14), kind=kLoop, calls=%fused_computation.4 | loop fusion | flops 12581888 | bytes 8392704 | tf_op jit(solution)/shard_map/reduce_sum | solution.py:18
  94.9 10.3 %multiply_convert_fusion = bf16[1,1024,4096]{2,1,0:T(8,128)(2,1)} fusion(bf16[1,1024,4096]{2,1,0:T(8,128)(2,1)} %param.14, f32[4096]{0:T(1024)S(1)} %bitcast.80, f32[1024]{0:T(1024)S(1)} %add_rsqrt_fusion), kind=kLoop, calls=%fused_computation.7 | loop fusion | flops 16777216 | bytes 16797696 | tf_op jit(solution)/shard_map/convert_element_type | solution.py:91
  105.3 33.9 %all-gather.10.cloned.1.call-done = bf16[1,4096,1024]{2,1,0:T(8,128)(2,1)} async-done(((bf16[1,512,1024]{2,1,0:T(8,128)(2,1)}), bf16[1,4096,1024]{2,1,0:T(8,128)(2,1)}) %all-gather.10.cloned.1.call-update) | async-done | bytes 8388624 | tf_op jit(solution)/shard_map/all_gather | solution.py:88
  139.2 12.2 %copy.37 = bf16[1024,4096]{1,0:T(8,128)(2,1)} copy(bf16[1024,4096]{0,1:T(8,128)(2,1)} %bitcast.72) | data formatting | bytes 16777216 | tf_op jit(solution)/shard_map/dot_general | solution.py:94
  151.4 113.1 %all-gather.12.cloned.1.call-done = bf16[1,4096,1024]{2,1,0:T(8,128)(2,1)} async-done(((bf16[1,512,1024]{2,1,0:T(8,128)(2,1)}), bf16[1,4096,1024]{2,1,0:T(8,128)(2,1)}) %all-gather.12.cloned.1.call-update) | async-done | bytes 8388624 | tf_op jit(solution)/shard_map/all_gather | solution.py:89
  264.5 14.1 %convert_bitcast_fusion = bf16[128,8,8,128]{3,1,2,0:T(8,128)(2,1)S(1)} fusion(bf16[1,4096,1024]{2,1,0:T(8,128)(2,1)} %all-gather.12.cloned.1.call-done, f32[4096]{0:T(1024)S(1)} %bitcast.81, f32[1024]{0:T(1024)S(1)} %add_rsqrt_fusion, bf16[1,1024,4096]{2,1,0:T(8,128)(2,1)} %param.14), kind=kOutput, calls=%fused_computation.28 | convolution fusion | flops 8607760384 | bytes 18894848 | tf_op jit(solution)/shard_map/dot_general | solution.py:95
  278.7 0.6 copy.45
  279.3 8.8 %fusion.89 = f32[2,512,8,128]{1,3,2,0:T(8,128)S(1)} fusion(bf16[2,512,4096,1]{2,1,3,0:T(8,128)(2,1)S(1)} %bitcast.73, bf16[8,128,4096,1]{2,1,0,3:T(8,128)(2,1)S(1)} %bitcast.74), kind=kOutput, calls=%fused_computation.95 | convolution fusion | flops 8589934592 | bytes 20971520 | tf_op jit(solution)/shard_map/dot_general | solution.py:94
  288.2 2.1 subtract_convert_fusion
  290.3 2.1 fusion.84
  292.9 9.2 %all_to_all.29 = bf16[2,8,512]{2,0,1:T(2,128)(2,1)S(1)} all-to-all(bf16[2,8,512]{2,0,1:T(2,128)(2,1)S(1)} %copy.40), channel_id=1, replica_groups=mesh['judge'=4,'fsdp'=8] {'fsdp'}, dimensions={1} | all-to-all | bytes 32768 | tf_op jit(solution)/shard_map/all_to_all | solution.py:119
  302.1 3.6 fusion.15
  305.7 26.3 %all-gather.4 = bf16[1,4096]{1,0:T(2,128)(2,1)S(1)} all-gather(bf16[1,512]{1,0:T(2,128)(2,1)S(1)} %copy-done.4), channel_id=6, replica_groups=mesh['judge'=4,'fsdp'=8] {'fsdp'}, dimensions={1}, use_global_device_ids=true | all-gather | bytes 9216 | tf_op jit(solution)/shard_map/all_gather | solution.py:82
  332.1 41.7 %all-reduce.4.cloned.1.call-done = f32[16,4096]{1,0:T(8,128)} async-done(((f32[16,4096]{1,0:T(8,128)}), f32[16,4096]{1,0:T(8,128)}) %all-reduce.4.cloned.1.call-update) | async-done | bytes 262160 | tf_op jit(solution)/shard_map/psum | solution.py:120
  373.8 1.1 multiply_reduce_fusion.1
  374.9 7.2 %fusion.8 = f32[16,1792]{1,0:T(8,128)S(1)} fusion(bf16[1,4096,1792]{2,1,0:T(8,128)(2,1)} %param.23, f32[16,4096]{1,0:T(8,128)S(1)} %get-tuple-element.9, f32[4096]{0:T(1024)S(1)} %bitcast.77, f32[16]{0:T(128)S(1)} %add_rsqrt_fusion.2), kind=kOutput, calls=%fused_computation.12 | convolution fusion | flops 235077632 | bytes 15073344 | tf_op jit(solution)/shard_map/dot_general | solution.py:125
  382.1 14.4 %fusion.4 = f32[16,4096]{1,0:T(8,128)} fusion(bf16[1,1792,4096]{2,1,0:T(8,128)(2,1)} %param.25, bf16[1,4096,1792]{2,1,0:T(8,128)(2,1)} %param.24, f32[16,1792]{1,0:T(8,128)S(1)} %fusion.8, f32[16,4096]{1,0:T(8,128)S(1)} %get-tuple-element.9, f32[4096]{0:T(1024)S(1)} %bitcast.78, f32[16]{0:T(128)S(1)} %add_rsqrt_fusion.2), kind=kOutput, calls=%fused_computation.8 | convolution fusion | flops 470130688 | bytes 30015552 | tf_op jit(solution)/shard_map/dot_general | solution.py:128
  396.5 26.0 %all-gather.5 = bf16[1,4096]{1,0:T(2,128)(2,1)S(1)} all-gather(bf16[1,512]{1,0:T(2,128)(2,1)S(1)} %copy-done.5), channel_id=7, replica_groups=mesh['judge'=4,'fsdp'=8] {'fsdp'}, dimensions={1}, use_global_device_ids=true | all-gather | bytes 9216 | tf_op jit(solution)/shard_map/all_gather | solution.py:83
  422.5 44.0 %all-reduce.6.cloned.1.call-done = f32[16,4096]{1,0:T(8,128)} async-done(((f32[16,4096]{1,0:T(8,128)}), f32[16,4096]{1,0:T(8,128)}) %all-reduce.6.cloned.1.call-update) | async-done | bytes 262160 | tf_op jit(solution)/shard_map/psum | solution.py:129
  466.5 1.1 multiply_reduce_fusion
  468.2 10.5 %all-reduce = (f32[16]{0:T(128)S(1)}, f32[16,512]{1,0:T(8,128)S(1)}) all-reduce(f32[16]{0:T(128)S(1)} %convolution_bitcast_fusion, f32[16,512]{1,0:T(8,128)S(1)} %constant_dynamic-slice_fusion), channel_id=1, replica_groups=mesh['judge'=4,'fsdp'=8] {'judge'}, use_global_device_ids=true, to_apply=%region_8.9 | all-reduce | flops 8208 | bytes 65664 | tf_op jit(solution)/shard_map/psum | solution.py:134
  479.6 0.9 fusion.60
  (52 shorter events, 3.6 us)
Async XLA Ops:
  7.2 460.6 %copy-start = (f32[1,4096]{1,0:T(1,128)S(1)}, f32[1,4096]{1,0:T(1,128)}, u32[]{:S(2)}) copy-start(f32[1,4096]{1,0:T(1,128)} %param.27) | copy-start | bytes 49156
  7.2 73.5 %copy-start.6 = (s32[16]{0:T(128)S(1)}, s32[16]{0:T(128)}, u32[]{:S(2)}) copy-start(s32[16]{0:T(128)} %param.15) | copy-start | bytes 196
  7.2 132.0 %all-gather.10.cloned.1.call-start = ((), (), s32[]{:S(2)}) async-start(), calls=%async_computation.4 | async-start | bytes 9437184 | tf_op jit(solution)/shard_map/all_gather | solution.py:88
  7.9 256.6 %all-gather.12.cloned.1.call-start = ((), (), s32[]{:S(2)}) async-start(), calls=%async_computation.5 | async-start | bytes 9437184 | tf_op jit(solution)/shard_map/all_gather | solution.py:89
  85.0 20.3 %all-to-all-start = ((bf16[8,2,512]{2,1,0:T(2,128)(2,1)}), bf16[8,2,512]{2,1,0:T(2,128)(2,1)S(1)}, u32[]{:S(2)}, u32[]{:S(2)}) async-start(bf16[8,2,512]{2,1,0:T(2,128)(2,1)} %convert_element_type.75), calls=%async_computation | async-start | bytes 32768 | tf_op jit(solution)/shard_map/all_to_all | solution.py:107
  89.0 284.8 %all-reduce.4.cloned.1.call-start = ((), (), s32[]{:S(2)}) async-start(), calls=%async_computation.2 | async-start | bytes 524288 | tf_op jit(solution)/shard_map/psum | solution.py:120
  264.5 14.8 %copy-start.1 = (bf16[1,1024,4096]{2,1,0:T(8,128)(2,1)S(1)}, bf16[1,1024,4096]{2,1,0:T(8,128)(2,1)}, u32[]{:S(2)}) copy-start(bf16[1,1024,4096]{2,1,0:T(8,128)(2,1)} %multiply_convert_fusion) | copy-start | bytes 25165828
  264.5 14.8 %copy-start.2 = (bf16[1024,4096]{1,0:T(8,128)(2,1)S(1)}, bf16[1024,4096]{1,0:T(8,128)(2,1)}, u32[]{:S(2)}) copy-start(bf16[1024,4096]{1,0:T(8,128)(2,1)} %copy.37) | copy-start | bytes 25165828
  288.2 17.6 %copy-start.4 = (bf16[1,512]{1,0:T(2,128)(2,1)S(1)}, bf16[1,512]{1,0:T(2,128)(2,1)}, u32[]{:S(2)}) copy-start(bf16[1,512]{1,0:T(2,128)(2,1)} %param.22) | copy-start | bytes 3076
  305.7 160.9 %all-reduce.6.cloned.1.call-start = ((), (), s32[]{:S(2)}) async-start(), calls=%async_computation.3 | async-start | bytes 524288 | tf_op jit(solution)/shard_map/psum | solution.py:129
  382.1 14.4 %copy-start.5 = (bf16[1,512]{1,0:T(2,128)(2,1)S(1)}, bf16[1,512]{1,0:T(2,128)(2,1)}, u32[]{:S(2)}) copy-start(bf16[1,512]{1,0:T(2,128)(2,1)} %param.26) | copy-start | bytes 3076
  382.1 96.6 %copy-start.3 = (s32[16]{0:T(128)S(1)}, s32[16]{0:T(128)}, u32[]{:S(2)}) copy-start(s32[16]{0:T(128)} %param.16) | copy-start | bytes 196
Sparse Core Ops, SparseCore 0:
  10.2 129.0 all-gather.9
  141.3 123.1 all-gather.11
  305.8 67.9 all-reduce.3
  396.6 69.8 all-reduce.5
where the time goes:
time: 488 us; the launch traced here: 487 us
  waiting for transfers between devices  234 us (48%)
  blocking collectives  132 us (27%)
  matrix products  55.4 us (11%)
  local copies, waits for them, and re-layouts  25.1 us (5%)
  other arithmetic  22.7 us (5%)
  between operations  14 us (3%)
    all_gather x1, waiting for transfers between devices, body(): lax.all_gather(w_value[0], 'fsdp', axis=0, tiled=True)  113 us
    psum x1, waiting for transfers between devices, body(): down = lax.psum(down_terms, 'fsdp')  44 us
    psum x1, waiting for transfers between devices, body(): lax.psum(jnp.dot(head_rows, w_out[0], preferred_element_type=jnp.float32)...  41.7 us
    all_gather x1, waiting for transfers between devices, body(): lax.all_gather(w_key[0], 'fsdp', axis=0, tiled=True)  33.9 us
    all_gather x1, blocking collectives, body(): lax.all_gather(own_last, 'fsdp', axis=0, tiled=True)  31.3 us
    all_gather x1, blocking collectives, body(): lax.all_gather(attn_gain[0], 'fsdp', axis=0, tiled=True)  28.3 us
    all_gather x1, blocking collectives, body(): lax.all_gather(mlp_gain[0], 'fsdp', axis=0, tiled=True)  26.3 us
    all_gather x1, blocking collectives, body(): lax.all_gather(final_gain[0], 'fsdp', axis=0, tiled=True)  26 us
  transfers between devices with their start and end apart: 5, of which 4 were waited for; matrix products, arithmetic and copies ran while one was open for 9% of the time, Pallas kernels for 0%

commit v1 on v0

v1 whole, which is shorter than its diff:
```python
import functools
import math

import jax
import jax.numpy as jnp
from jax import lax
from jax.experimental import pallas as pl
from jax.experimental.pallas import tpu as pltpu
from jax.sharding import PartitionSpec as P

KV_HEADS = 8
HEAD_DIM = 128
LEN = 512


EPS = 1e-05
ROPE_BASE = 500000.0


def row_scale(v):
    return lax.rsqrt(jnp.mean(v * v, axis=-1, keepdims=True) + EPS)


def angles(position):
    half = HEAD_DIM // 2
    freq = jnp.exp(jnp.arange(half, dtype=jnp.float32) * (-2.0 * math.log(ROPE_BASE) / HEAD_DIM))
    turned = position[..., None] * freq
    return (jnp.cos(turned), jnp.sin(turned))


def rotate(v, cosine, sine):
    half = HEAD_DIM // 2
    first = v[..., :half]
    second = v[..., half:]
    return jnp.concatenate(
        [first * cosine - second * sine, second * cosine + first * sine], axis=-1
    )


def remaining_candidates(judge_panel, duplicate_group_index, duplicate_groups):
    same = duplicate_group_index[:, None] == duplicate_group_index[None, :]
    top = jnp.max(jnp.where(same, judge_panel[None, :], -1e30), axis=1)
    expo = jnp.exp(judge_panel - top)
    total = jnp.sum(jnp.where(same, expo[None, :], 0.0), axis=1)
    weight_values = expo / total
    panel_member = (
        duplicate_group_index[:, None] == jnp.arange(duplicate_groups, dtype=jnp.int32)[None, :]
    ).astype(jnp.float32)
    return (weight_values, panel_member)


def peer_of(me, k, n):
    return lax.rem(me + k, n)


def greet(axes):
    barrier = pltpu.get_barrier_semaphore()
    total = 0
    for axis, n in axes:
        me = lax.axis_index(axis)

        def signal(k, carry, axis=axis, n=n, me=me):
            pl.semaphore_signal(
                barrier,
                inc=1,
                device_id={axis: peer_of(me, k, n)},
                device_id_type=pl.DeviceIdType.MESH,
            )
            return carry

        lax.fori_loop(1, n, signal, 0)
        total += n - 1
    pl.semaphore_wait(barrier, total)


def remote(src, dst, send_sem, recv_sem, axis, peer):
    return pltpu.make_async_remote_copy(
        src_ref=src,
        dst_ref=dst,
        send_sem=send_sem,
        recv_sem=recv_sem,
        device_id={axis: peer},
        device_id_type=pl.DeviceIdType.MESH,
    )


def start_all(axis, n, source, dst, sems):
    me = lax.axis_index(axis)

    def one(k, carry):
        peer = peer_of(me, k, n)
        remote(source(peer), dst.at[me], sems.at[0, k], sems.at[1, k], axis, peer).start()
        return carry

    lax.fori_loop(1, n, one, 0)


def recv_all(axis, n, dst, sems):
    me = lax.axis_index(axis)

    def one(k, carry):
        sender = peer_of(me, n - k, n)
        block = dst.at[sender]
        remote(block, block, sems.at[0, k], sems.at[1, k], axis, sender).wait_recv()
        return carry

    lax.fori_loop(1, n, one, 0)


def sent_all(axis, n, dst, sems):
    me = lax.axis_index(axis)

    def one(k, carry):
        block = dst.at[me]
        remote(block, block, sems.at[0, k], sems.at[1, k], axis, peer_of(me, k, n)).wait_send()
        return carry

    lax.fori_loop(1, n, one, 0)


def attend_kernel(
    n,
    seq_dev,
    own_len,
    tokens,
    w_query,
    w_key,
    w_value,
    last_pack,
    gain_pack,
    q_cos,
    q_sin,
    k_cos,
    k_sin,
    mixed_out,
    last_out,
    gain_out,
    wk,
    tn,
    acc,
    wq,
    wv,
    tok,
    lp,
    gp,
    xl,
    gain,
    qp,
    qr,
    qs,
    pr,
    pt,
    ptr,
    part,
    got,
    ring_send,
    ring_recv,
    local_sem,
    tok_sem,
    last_sem,
    gain_sem,
    q_sem,
    pt_sem,
    got_sem,
):
    axis = "fsdp"
    me = lax.axis_index(axis)
    rows = w_key.shape[0]
    half_cols = wk.shape[-1]
    sub = rows // 2
    width = tokens.shape[1]
    tok_dev = tokens.shape[0]
    cands = xl.shape[0]
    half_n = n // 2
    odd = lax.rem(me, 2)
    pos = (1 - odd) * (me // 2) + odd * (n - 1 - me // 2)

    def at_pos(p):
        p = lax.rem(p, n)
        back = p // half_n
        return (1 - back) * (2 * p) + back * (2 * (n - 1 - p) + 1)

    after = at_pos(pos + 1)
    before = at_pos(pos + n - 1)

    def copies(step, direction, j):
        if direction == 0:
            owner, target = at_pos(pos + n - step), after
        else:
            owner, target = at_pos(pos + step), before
        piece = wk.at[owner, direction, pl.ds(j * sub, sub), :]
        sems = (ring_send.at[direction, j, step], ring_recv.at[direction, j, step])
        return piece, target, sems

    own_key = [
        pltpu.make_async_copy(
            w_key.at[:, pl.ds(d * half_cols, half_cols)], wk.at[me, d], local_sem.at[d]
        )
        for d in range(2)
    ]
    for copy in own_key:
        copy.start()
    query_copy = pltpu.make_async_copy(w_query, wq, local_sem.at[2])
    value_copy = pltpu.make_async_copy(w_value, wv, local_sem.at[3])
    chunk = tok.shape[1]
    chunks = tok_dev // chunk

    def tok_copy(c):
        return pltpu.make_async_copy(
            tokens.at[pl.ds(c * chunk, chunk), :], tok.at[lax.rem(c, 2)], tok_sem.at[lax.rem(c, 2)]
        )

    tok_copy(0).start()
    greet([(axis, n)])
    start_all(axis, n, lambda peer: last_pack, lp, last_sem)
    start_all(axis, n, lambda peer: gain_pack, gp, gain_sem)
    for copy in own_key:
        copy.wait()
    for j in range(2):
        for d in range(2):
            piece, target, sems = copies(0, d, j)
            remote(piece, piece, *sems, axis, target).start()
    query_copy.start()
    value_copy.start()
    lp[me] = last_pack[...]
    gp[me] = gain_pack[...]
    recv_all(axis, n, gp, gain_sem)
    for o in range(n):
        gain[0:1, o * rows : (o + 1) * rows] = gp[o, 0:1, :]

    def normalise(c, carry):
        @pl.when(c < chunks - 1)
        def _():
            tok_copy(c + 1).start()

        tok_copy(c).wait()
        v = tok[lax.rem(c, 2)].astype(jnp.float32)
        v = (v * row_scale(v) * gain[...]).astype(jnp.bfloat16)
        for o in range(n):
            tn[o, pl.ds(pl.multiple_of(c * chunk, chunk), chunk), :] = v[:, o * rows : (o + 1) * rows]
        return carry

    lax.fori_loop(0, chunks, normalise, 0)
    tile = 256

    def multiply(owner, d, first):
        def one(i, carry):
            r = pl.ds(pl.multiple_of(i * tile, tile), tile)
            term = jnp.dot(tn[owner, r, :], wk[owner, d], preferred_element_type=jnp.float32)
            if first:
                acc[d, r, :] = term
            else:
                acc[d, r, :] += term
            return carry

        lax.fori_loop(0, tok_dev // tile, one, 0)

    def take(step):
        for j in range(2):
            for d in range(2):
                piece, target, sems = copies(step, d, j)
                owner = at_pos(pos + n - 1 - step) if d == 0 else at_pos(pos + 1 + step)
                arrived = wk.at[owner, d, pl.ds(j * sub, sub), :]
                remote(arrived, arrived, *sems, axis, target).wait_recv()

                @pl.when(step < n - 2)
                def _():
                    piece, target, sems = copies(step + 1, d, j)
                    remote(piece, piece, *sems, axis, target).start()

    take(0)
    for d in range(2):
        multiply(me, d, True)
    recv_all(axis, n, lp, last_sem)
    pack_width = lp.shape[2]
    blocks = width // pack_width
    for o in range(n):
        for b in range(blocks):
            xl[o * seq_dev : (o + 1) * seq_dev, b * pack_width : (b + 1) * pack_width] = lp[
                o, b * seq_dev : (b + 1) * seq_dev, :
            ]
    last_out[...] = xl[...]
    gain_out[...] = gp[...]
    query_copy.wait()
    v = xl[...]
    q = jnp.dot(
        (v * row_scale(v) * gain[...]).astype(jnp.bfloat16),
        wq[...],
        preferred_element_type=jnp.float32,
    )
    heads_dev = q.shape[1] // HEAD_DIM
    qp[...] = jnp.zeros_like(qp)
    for h in range(heads_dev):
        one = q[:, h * HEAD_DIM : (h + 1) * HEAD_DIM]
        one = one * q_cos[...] + pltpu.roll(one, HEAD_DIM // 2, 1) * q_sin[...]
        one = one.astype(jnp.bfloat16).astype(jnp.float32)
        for o in range(n):
            qp[o, h * seq_dev : (h + 1) * seq_dev, :] = one[o * seq_dev : (o + 1) * seq_dev, :]
    start_all(axis, n, lambda peer: qp.at[peer], qr, q_sem)
    qr[me] = qp[me]

    def use(step):
        multiply(at_pos(pos + n - 1 - step), 0, False)
        multiply(at_pos(pos + 1 + step), 1, False)

    use(0)

    def ring(step, carry):
        take(step)
        use(step)
        return carry

    lax.fori_loop(1, n - 1, ring, 0)
    recv_all(axis, n, qr, q_sem)
    groups = width // HEAD_DIM // KV_HEADS
    qs[...] = jnp.zeros_like(qs)
    for head in range(KV_HEADS * groups):
        for s in range(seq_dev):
            row = (head % heads_dev) * seq_dev + s
            qs[s, head // groups, head % groups : head % groups + 1, :] = qr[
                head // heads_dev, row : row + 1, :
            ]
    per_half = half_cols // HEAD_DIM
    for s in range(seq_dev):
        valid = lax.broadcasted_iota(jnp.int32, (8, LEN), 1) < own_len[s]
        for k in range(KV_HEADS):
            key = acc[
                k // per_half,
                s * LEN : (s + 1) * LEN,
                k % per_half * HEAD_DIM : (k % per_half + 1) * HEAD_DIM,
            ]
            key = (key * k_cos[...] + pltpu.roll(key, HEAD_DIM // 2, 1) * k_sin[...]).astype(
                jnp.bfloat16
            )
            scores = lax.dot_general(
                qs[s, k].astype(jnp.bfloat16),
                key,
                (((1,), (1,)), ((), ())),
                preferred_element_type=jnp.float32,
            ) * HEAD_DIM ** (-0.5)
            scores = jnp.where(valid, scores, -1e30)
            expo = jnp.exp(scores - jnp.max(scores, axis=-1, keepdims=True))
            pr[s, k] = expo / jnp.sum(expo, axis=-1, keepdims=True)
    each = KV_HEADS * 8
    for s in range(seq_dev):
        probs = pr[s].reshape(each, LEN).astype(jnp.bfloat16)

        def spread(o, carry, s=s, probs=probs):
            one = jnp.dot(
                probs, tn[o, s * LEN : (s + 1) * LEN, :], preferred_element_type=jnp.float32
            ).astype(jnp.bfloat16)
            pt[o, s * each : (s + 1) * each, :] = one
            return carry

        lax.fori_loop(0, n, spread, 0)
    start_all(axis, n, lambda peer: pt.at[peer], ptr, pt_sem)
    ptr[me] = pt[me]
    value_copy.wait()
    recv_all(axis, n, ptr, pt_sem)
    kpd = max(1, KV_HEADS // n)

    def project(src, carry):
        full = jnp.dot(ptr[src], wv[...], preferred_element_type=jnp.float32)
        for o in range(n):
            for i in range(kpd):
                k = o * heads_dev // groups + i
                for s in range(seq_dev):
                    part[o, i * seq_dev + s, src] = full[
                        s * each + k * 8 : s * each + (k + 1) * 8, k * HEAD_DIM : (k + 1) * HEAD_DIM
                    ]
        return carry

    lax.fori_loop(0, n, project, 0)
    start_all(axis, n, lambda peer: part.at[peer], got, got_sem)
    got[me] = part[me]
    recv_all(axis, n, got, got_sem)
    total = got[0]
    for o in range(1, n):
        total = total + got[o]
    mixed_out[...] = total

    def drain(step, carry):
        for j in range(2):
            for d in range(2):
                piece, target, sems = copies(step, d, j)
                remote(piece, piece, *sems, axis, target).wait_send()
        return carry

    lax.fori_loop(0, n - 1, drain, 0)
    sent_all(axis, n, lp, last_sem)
    sent_all(axis, n, gp, gain_sem)
    sent_all(axis, n, qr, q_sem)
    sent_all(axis, n, ptr, pt_sem)
    sent_all(axis, n, got, got_sem)


def feed_kernel(
    n,
    judges,
    mixed,
    last_cols,
    gains,
    gain_final,
    reward,
    w_out,
    w_gate,
    w_up,
    w_down,
    feat_out,
    score_out,
    wo,
    wg,
    wu,
    wd,
    send_a,
    recv_a,
    full,
    m_norm,
    send_d,
    recv_d,
    stats,
    feats,
    scores,
    local_sem,
    gate_sem,
    up_sem,
    a_sem,
    g_sem,
    d_sem,
    s_sem,
    f_sem,
    c_sem,
):
    axis = "fsdp"
    me = lax.axis_index(axis)
    judge = lax.axis_index("judge")
    rows = w_out.shape[0]
    width = w_out.shape[1]
    cands = mixed.shape[0]
    hidden = w_gate.shape[1]
    out_copy = pltpu.make_async_copy(w_out, wo, local_sem.at[0])
    down_copy = pltpu.make_async_copy(w_down, wd, local_sem.at[1])
    out_copy.start()

    def columns(o):
        return pl.ds(pl.multiple_of(o * rows, rows), rows)

    def part_copies(o):
        return (
            pltpu.make_async_copy(w_gate.at[columns(o), :], wg.at[columns(o), :], gate_sem.at[o]),
            pltpu.make_async_copy(w_up.at[columns(o), :], wu.at[columns(o), :], up_sem.at[o]),
        )

    def fetch(o, carry):
        for copy in part_copies(o):
            copy.start()
        return carry

    lax.fori_loop(0, n, fetch, 0)
    down_copy.start()
    greet([(axis, n), ("judge", judges)])
    out_copy.wait()

    def attn_part(o, carry):
        send_a[o] = jnp.dot(mixed[...], wo[:, columns(o)], preferred_element_type=jnp.float32)
        return carry

    lax.fori_loop(0, n, attn_part, 0)
    start_all(axis, n, lambda peer: send_a.at[peer], recv_a, a_sem)
    recv_a[me] = send_a[me]
    recv_all(axis, n, recv_a, a_sem)
    own = recv_a[0]
    for o in range(1, n):
        own = own + recv_a[o]
    own = last_cols[...] + own
    full[me] = own
    start_all(axis, n, lambda peer: full.at[me], full, g_sem)
    recv_all(axis, n, full, g_sem)
    square = full[0] * full[0]
    for o in range(1, n):
        square = square + full[o] * full[o]
    scale = lax.rsqrt(jnp.sum(square, axis=-1, keepdims=True) / width + EPS)
    for o in range(n):
        m_norm[o] = (full[o] * scale * gains[o, 1:2, :]).astype(jnp.bfloat16)

    def widen(o, carry):
        for copy in part_copies(o):
            copy.wait()
        one = m_norm[o]
        gate = jnp.dot(one, wg[columns(o), :], preferred_element_type=jnp.float32)
        up = jnp.dot(one, wu[columns(o), :], preferred_element_type=jnp.float32)
        return (carry[0] + gate, carry[1] + up)

    zero = jnp.zeros((cands, hidden), jnp.float32)
    gate, up = lax.fori_loop(0, n, widen, (zero, zero))
    act = (gate / (1.0 + jnp.exp(-gate)) * up).astype(jnp.bfloat16)
    down_copy.wait()

    def down_part(k, carry):
        o = peer_of(me, k, n)
        send_d[o] = jnp.dot(act, wd[:, columns(o)], preferred_element_type=jnp.float32)

        remote(send_d.at[o], recv_d.at[me], d_sem.at[0, k], d_sem.at[1, k], axis, o).start()
        return carry

    lax.fori_loop(1, n, down_part, 0)
    recv_d[me] = jnp.dot(act, wd[:, columns(me)], preferred_element_type=jnp.float32)
    recv_all(axis, n, recv_d, d_sem)
    mlp = recv_d[0]
    for o in range(1, n):
        mlp = mlp + recv_d[o]
    mlp = full[me] + mlp
    feat = mlp * gain_final[...]
    lane = lax.broadcasted_iota(jnp.int32, (cands, HEAD_DIM), 1)
    stats[me] = jnp.where(
        lane == 0,
        jnp.sum(mlp * mlp, axis=-1, keepdims=True),
        jnp.sum(feat * reward[...], axis=-1, keepdims=True),
    )
    start_all(axis, n, lambda peer: stats.at[me], stats, s_sem)
    recv_all(axis, n, stats, s_sem)
    total = stats[0]
    for o in range(1, n):
        total = total + stats[o]
    scale = lax.rsqrt(total[:, 0:1] / width + EPS)
    feats[judge] = feat * scale
    scores[judge] = total * scale
    start_all("judge", judges, lambda peer: feats.at[judge], feats, f_sem)
    start_all("judge", judges, lambda peer: scores.at[judge], scores, c_sem)
    recv_all("judge", judges, feats, f_sem)
    recv_all("judge", judges, scores, c_sem)
    feat = feats[0]
    score = scores[0]
    for j in range(1, judges):
        feat = feat + feats[j]
        score = score + scores[j]
    feat_out[...] = feat
    score_out[...] = score
    sent_all(axis, n, recv_a, a_sem)
    sent_all(axis, n, full, g_sem)
    sent_all(axis, n, recv_d, d_sem)
    sent_all(axis, n, stats, s_sem)
    sent_all("judge", judges, feats, f_sem)
    sent_all("judge", judges, scores, c_sem)


def body(
    hidden,
    lengths,
    duplicate_group_index,
    attn_gain,
    w_query,
    w_key,
    w_value,
    w_out,
    mlp_gain,
    w_gate,
    w_up,
    w_down,
    final_gain,
    reward_head,
):
    judges = lax.axis_size("judge")
    n = lax.axis_size("fsdp")
    me = lax.axis_index("fsdp")
    tokens = hidden[0]
    tok_dev, width = tokens.shape
    seq_dev = tok_dev // LEN
    cands = lengths.shape[0]
    duplicate_groups = cands // 4
    heads = width // HEAD_DIM
    groups = heads // KV_HEADS
    cols = width // n
    heads_dev = cols // HEAD_DIM
    kvw = w_key.shape[2]
    f32, bf16 = jnp.float32, jnp.bfloat16
    own_len = lax.dynamic_slice_in_dim(lengths, me * seq_dev, seq_dev)
    own_last = jnp.concatenate(
        [
            lax.dynamic_slice_in_dim(tokens, s * LEN + own_len[s] - 1, 1, 0)
            for s in range(seq_dev)
        ],
        axis=0,
    ).astype(f32)
    pack_width = seq_dev * width // 8
    last_pack = own_last.reshape(seq_dev, width // pack_width, pack_width)
    last_pack = last_pack.transpose(1, 0, 2).reshape(8, pack_width)
    gain_pack = jnp.concatenate(
        [attn_gain, mlp_gain, final_gain, jnp.zeros((5, cols), bf16)], axis=0
    ).astype(f32)

    def table(position):
        cosine, sine = angles(position)
        return (
            jnp.concatenate([cosine, cosine], axis=-1),
            jnp.concatenate([-sine, sine], axis=-1),
        )

    q_cos, q_sin = table((lengths - 1).astype(f32))
    k_cos, k_sin = table(jnp.arange(LEN, dtype=f32))
    kpd = max(1, KV_HEADS // n)
    q_rows = max(8, heads_dev * seq_dev)
    each = KV_HEADS * 8
    vmem = pl.BlockSpec(memory_space=pltpu.VMEM)
    anywhere = pl.BlockSpec(memory_space=pl.ANY)
    dma = pltpu.SemaphoreType.DMA
    mixed_pack, x_last, gains = pl.pallas_call(
        functools.partial(attend_kernel, n, seq_dev),
        out_shape=(
            jax.ShapeDtypeStruct((kpd * seq_dev, n, 8, HEAD_DIM), f32),
            jax.ShapeDtypeStruct((cands, width), f32),
            jax.ShapeDtypeStruct((n, 8, cols), f32),
        ),
        in_specs=[pl.BlockSpec(memory_space=pltpu.SMEM)] + [anywhere] * 4 + [vmem] * 6,
        out_specs=(vmem, vmem, vmem),
        scratch_shapes=[
            pltpu.VMEM((n, 2, cols, kvw // 2), bf16),
            pltpu.VMEM((n, tok_dev, cols), bf16),
            pltpu.VMEM((2, tok_dev, kvw // 2), f32),
            pltpu.VMEM((width, cols), bf16),
            pltpu.VMEM((cols, kvw), bf16),
            pltpu.VMEM((2, 128, width), bf16),
            pltpu.VMEM((n, 8, pack_width), f32),
            pltpu.VMEM((n, 8, cols), f32),
            pltpu.VMEM((cands, width), f32),
            pltpu.VMEM((1, width), f32),
            pltpu.VMEM((n, q_rows, HEAD_DIM), f32),
            pltpu.VMEM((n, q_rows, HEAD_DIM), f32),
            pltpu.VMEM((seq_dev, KV_HEADS, 8, HEAD_DIM), f32),
            pltpu.VMEM((seq_dev, KV_HEADS, 8, LEN), f32),
            pltpu.VMEM((n, seq_dev * each, cols), bf16),
            pltpu.VMEM((n, seq_dev * each, cols), bf16),
            pltpu.VMEM((n, kpd * seq_dev, n, 8, HEAD_DIM), f32),
            pltpu.VMEM((n, kpd * seq_dev, n, 8, HEAD_DIM), f32),
            dma((2, 2, n)),
            dma((2, 2, n)),
            dma((4,)),
            dma((2,)),
            dma((2, n)),
            dma((2, n)),
            dma((2, n)),
            dma((2, n)),
            dma((2, n)),
        ],
        compiler_params=pltpu.CompilerParams(
            collective_id=0, has_side_effects=True, vmem_limit_bytes=50 * 2**20
        ),
    )(
        own_len,
        tokens,
        w_query[0],
        w_key[0],
        w_value[0],
        last_pack,
        gain_pack,
        q_cos,
        q_sin,
        k_cos,
        k_sin,
    )
    mixed = mixed_pack.reshape(kpd, seq_dev, n, 8, HEAD_DIM)[:, :, :, :groups]
    mixed = mixed.transpose(2, 1, 0, 3, 4).reshape(cands, kpd * groups * HEAD_DIM).astype(bf16)
    first = lax.rem(me * heads_dev, groups) if heads_dev < groups else 0
    mixed = lax.dynamic_slice_in_dim(mixed, first * HEAD_DIM, cols, 1)
    last_cols = lax.dynamic_slice_in_dim(x_last, me * cols, cols, 1)
    reward = lax.dynamic_slice_in_dim(reward_head, me * cols, cols, 1)
    hidden_dev = w_gate.shape[2]
    total_cols, score_total = pl.pallas_call(
        functools.partial(feed_kernel, n, judges),
        out_shape=(
            jax.ShapeDtypeStruct((cands, cols), f32),
            jax.ShapeDtypeStruct((cands, HEAD_DIM), f32),
        ),
        in_specs=[vmem] * 5 + [anywhere] * 4,
        out_specs=(vmem, vmem),
        scratch_shapes=[
            pltpu.VMEM((cols, width), bf16),
            pltpu.VMEM((width, hidden_dev), bf16),
            pltpu.VMEM((width, hidden_dev), bf16),
            pltpu.VMEM((hidden_dev, width), bf16),
            pltpu.VMEM((n, cands, cols), f32),
            pltpu.VMEM((n, cands, cols), f32),
            pltpu.VMEM((n, cands, cols), f32),
            pltpu.VMEM((n, cands, cols), bf16),
            pltpu.VMEM((n, cands, cols), f32),
            pltpu.VMEM((n, cands, cols), f32),
            pltpu.VMEM((n, cands, HEAD_DIM), f32),
            pltpu.VMEM((judges, cands, cols), f32),
            pltpu.VMEM((judges, cands, HEAD_DIM), f32),
            dma((2,)),
            dma((n,)),
            dma((n,)),
            dma((2, n)),
            dma((2, n)),
            dma((2, n)),
            dma((2, n)),
            dma((2, judges)),
            dma((2, judges)),
        ],
        compiler_params=pltpu.CompilerParams(
            collective_id=1, has_side_effects=True, vmem_limit_bytes=60 * 2**20
        ),
    )(
        mixed,
        last_cols,
        gains,
        final_gain.astype(f32),
        reward,
        w_out[0],
        w_gate[0],
        w_up[0],
        w_down[0],
    )
    weight_values, panel_member = remaining_candidates(
        score_total[:, 1] / judges, duplicate_group_index, duplicate_groups
    )
    cluster_cols = jnp.dot(
        panel_member.T,
        weight_values[:, None] * (total_cols / judges),
        precision=lax.Precision.HIGHEST,
    )
    return (weight_values, cluster_cols)


def solution(mesh):
    in_specs = (
        P("judge", "fsdp", None),
        P(),
        P(),
        P("judge", "fsdp"),
        P("judge", None, "fsdp"),
        P("judge", "fsdp", None),
        P("judge", "fsdp", None),
        P("judge", "fsdp", None),
        P("judge", "fsdp"),
        P("judge", None, "fsdp"),
        P("judge", None, "fsdp"),
        P("judge", "fsdp", None),
        P("judge", "fsdp"),
        P("judge", None),
    )
    out_specs = (P(), P(None, "fsdp"))
    return jax.shard_map(body, mesh=mesh, in_specs=in_specs, out_specs=out_specs, check_vma=False)
```

time: 488 us -> 208 us (0.43)
  waiting for transfers between devices: 234 us -> 0 us
  Pallas kernels: 0 us -> 189 us
  blocking collectives: 132 us -> 0 us
  matrix products: 55.4 us -> 1.62 us
  local copies, waits for them, and re-layouts: 25.1 us -> 7.43 us
  other arithmetic: 22.7 us -> 6.15 us
  between operations: 14 us -> 3.33 us
    pallas_call x0 -> x2, Pallas kernels: none -> 189 us  [the longest x1 146 us: body(): pl.pallas_call(functools.partial(attend_kernel, n, seq_dev), out_shape=(j...]
    all_gather x2 -> x0, waiting for transfers between devices: 147 us -> none  [the longest x1 113 us: body(): lax.all_gather(w_value[0], 'fsdp', axis=0, tiled=True)]
    all_gather x4 -> x0, blocking collectives: 112 us -> none  [the longest x1 31.3 us: body(): lax.all_gather(own_last, 'fsdp', axis=0, tiled=True)]
    psum x2 -> x0, waiting for transfers between devices: 85.7 us -> none  [the longest x1 44 us: body(): down = lax.psum(down_terms, 'fsdp')]
    dot_general x9 -> x1, matrix products: 53.3 us -> 1.62 us  [body(): jnp.dot(panel_member.T, weight_values[:, None] * (total_cols / judges), p...]
    dot_general x2 -> x0, local copies, waits for them, and re-layouts: 18.6 us -> none  [the longest x1 12.2 us: body(): keys = jnp.dot(tok_norm, key_rows, preferred_element_type=jnp.float32)]
    psum x1 -> x0, blocking collectives: 10.5 us -> none  [body(): total_cols, score_total = lax.psum((feature_cols, score), 'judge')]
    all_to_all x1 -> x0, blocking collectives: 9.16 us -> none  [body(): lax.all_to_all(mixed, 'fsdp', split_axis=1, concat_axis=0, tiled=True)]
  transfers between devices with their start and end apart: 5 -> 0, of which waited for: 4 -> 0; matrix products, arithmetic and copies ran while one was open for 9% -> 0% of each run, Pallas kernels for 0% -> 0%
where the time goes in v1:
time: 208 us; the launch traced here: 207 us
  Pallas kernels  189 us (91%)
  local copies, waits for them, and re-layouts  7.43 us (4%)
  other arithmetic  6.15 us (3%)
  between operations  3.33 us (2%)
    pallas_call x1, Pallas kernels, body(): pl.pallas_call(functools.partial(attend_kernel, n, seq_dev), out_shape=(j...  146 us
    pallas_call x1, Pallas kernels, body(): pl.pallas_call(functools.partial(feed_kernel, n, judges), out_shape=(jax....  42.6 us

profile of v1, /device:TPU:0, one launch (start us, length us, event | category | flops | bytes accessed | tf_op | source)
XLA Modules:
  0.0 207.1 jit_solution(528863949868594459)
XLA Ops:
  0.6 0.0 copy-start
  0.6 0.7 dynamic_slice.15.own_len
  1.4 0.6 fusion.11
  4.6 0.9 constant_dynamic-slice_fusion.3
  5.6 1.0 fusion.2
  6.6 0.0 copy-start.4
  6.6 0.2 pad_maximum_fusion
  6.8 0.7 add_convert_fusion
  7.5 0.1 fusion.10
  7.6 0.1 pad_maximum_fusion.2
  7.7 0.1 pad.11.clone
  7.7 0.8 maximum_convert_fusion.gain_pack
  8.5 1.2 copy-done.1
  9.8 1.2 copy-done.2
  11.0 146.0 %shard_map.149 = (f32[2,8,8,128]{3,2,1,0:T(8,128)S(1)}, f32[16,4096]{1,0:T(8,128)S(1)}, f32[8,8,512]{2,1,0:T(8,128)S(1)}) custom-call(s32[2]{0:T(128)S(1)} %dynamic_slice.15.own_len, bf16[1024,4096]{1,0:T(8,128)(2,1)} %bitcast.33, bf16[4096,512]{1,0:T(8,128)(2,1)} %bitcast.34, bf16[512,1024]{1,0:T(8,128)(2,1)S(1)} %bitcast.28, ...), custom_call_target="tpu_custom_call" | custom-call | tf_op jit(solution)/shard_map/pallas_call | solution.py:607
  157.0 0.0 copy-start.3
  157.0 0.6 copy-done.3
  157.6 0.6 copy.27
  158.2 0.6 constant_dynamic-slice_fusion.1.last_cols
  158.9 0.6 constant_dynamic-slice_fusion.reward
  159.4 0.0 copy-done.4
  159.4 0.6 convert_element_type.21.gain_final
  160.0 42.6 %shard_map.150 = (f32[16,512]{1,0:T(8,128)}, f32[16,128]{1,0:T(8,128)}) custom-call(bf16[16,512]{1,0:T(8,128)(2,1)} %bitcast.36, f32[16,512]{1,0:T(8,128)} %constant_dynamic-slice_fusion.1.last_cols, f32[8,8,512]{2,1,0:T(8,128)} %copy-done.3, f32[1,512]{1,0:T(1,128)} %convert_element_type.21.gain_final, f32[1,512]{1,0:T(1,128)} %constant_dynamic-slice_fusion.reward, ...), custom_call_target="tpu_custom_call" | custom-call | tf_op jit(solution)/shard_map/pallas_call | solution.py:668
  202.6 0.9 fusion.8
  203.5 0.0 copy-done.5
  203.5 0.2 fusion.6
  203.7 0.2 fusion.7
  203.9 0.1 copy.24
  204.0 0.1 copy.23
  204.1 0.9 multiply_reduce_fusion
  204.9 1.6 fusion.3
  206.6 0.5 div.15
  (12 shorter events, 0.1 us)
Async XLA Ops:
  0.6 158.2 %copy-start = (f32[1,4096]{1,0:T(1,128)S(1)}, f32[1,4096]{1,0:T(1,128)}, u32[]{:S(2)}) copy-start(f32[1,4096]{1,0:T(1,128)} %param.27) | copy-start | bytes 49156
  6.6 152.9 %copy-start.4 = (bf16[1,512]{1,0:T(2,128)(2,1)S(1)}, bf16[1,512]{1,0:T(2,128)(2,1)}, u32[]{:S(2)}) copy-start(bf16[1,512]{1,0:T(2,128)(2,1)} %param.26) | copy-start | bytes 3076
  8.5 1.2 copy-start.1
  9.8 1.2 copy-start.2
  157.0 0.6 copy-start.3
  160.0 43.5 %copy-start.5 = (s32[16]{0:T(128)S(1)}, s32[16]{0:T(128)}, u32[]{:S(2)}) copy-start(s32[16]{0:T(128)} %param.16) | copy-start | bytes 196

commit v2 on v1

--- a/solution.py
+++ b/solution.py
@@ -151,6 +151,7 @@
     pr,
     pt,
     ptr,
+    proj,
     part,
     got,
     ring_send,
@@ -240,7 +241,6 @@
             tn[o, pl.ds(pl.multiple_of(c * chunk, chunk), chunk), :] = v[:, o * rows : (o + 1) * rows]
         return carry
 
-    lax.fori_loop(0, chunks, normalise, 0)
     tile = 256
 
     def multiply(owner, d, first):
@@ -268,9 +268,18 @@
                     piece, target, sems = copies(step + 1, d, j)
                     remote(piece, piece, *sems, axis, target).start()
 
+    def use(step):
+        multiply(at_pos(pos + n - 1 - step), 0, False)
+        multiply(at_pos(pos + 1 + step), 1, False)
+
     take(0)
+    lax.fori_loop(0, chunks, normalise, 0)
+    take(1)
     for d in range(2):
         multiply(me, d, True)
+    use(0)
+    use(1)
+    take(2)
     recv_all(axis, n, lp, last_sem)
     pack_width = lp.shape[2]
     blocks = width // pack_width
@@ -298,31 +307,24 @@
             qp[o, h * seq_dev : (h + 1) * seq_dev, :] = one[o * seq_dev : (o + 1) * seq_dev, :]
     start_all(axis, n, lambda peer: qp.at[peer], qr, q_sem)
     qr[me] = qp[me]
-
-    def use(step):
-        multiply(at_pos(pos + n - 1 - step), 0, False)
-        multiply(at_pos(pos + 1 + step), 1, False)
-
-    use(0)
+    use(2)
 
     def ring(step, carry):
         take(step)
         use(step)
         return carry
 
-    lax.fori_loop(1, n - 1, ring, 0)
+    lax.fori_loop(3, n - 1, ring, 0)
     recv_all(axis, n, qr, q_sem)
     groups = width // HEAD_DIM // KV_HEADS
-    qs[...] = jnp.zeros_like(qs)
     for head in range(KV_HEADS * groups):
         for s in range(seq_dev):
             row = (head % heads_dev) * seq_dev + s
-            qs[s, head // groups, head % groups : head % groups + 1, :] = qr[
-                head // heads_dev, row : row + 1, :
-            ]
+            slot = s * groups + head % groups
+            qs[head // groups, slot : slot + 1, :] = qr[head // heads_dev, row : row + 1, :]
     per_half = half_cols // HEAD_DIM
     for s in range(seq_dev):
-        valid = lax.broadcasted_iota(jnp.int32, (8, LEN), 1) < own_len[s]
+        valid = lax.broadcasted_iota(jnp.int32, (seq_dev * groups, LEN), 1) < own_len[s]
         for k in range(KV_HEADS):
             key = acc[
                 k // per_half,
@@ -333,40 +335,49 @@
                 jnp.bfloat16
             )
             scores = lax.dot_general(
-                qs[s, k].astype(jnp.bfloat16),
+                qs[k].astype(jnp.bfloat16),
                 key,
                 (((1,), (1,)), ((), ())),
                 preferred_element_type=jnp.float32,
             ) * HEAD_DIM ** (-0.5)
             scores = jnp.where(valid, scores, -1e30)
             expo = jnp.exp(scores - jnp.max(scores, axis=-1, keepdims=True))
-            pr[s, k] = expo / jnp.sum(expo, axis=-1, keepdims=True)
-    each = KV_HEADS * 8
+            probs = expo / jnp.sum(expo, axis=-1, keepdims=True)
+            pr[s, k * groups : (k + 1) * groups, :] = probs[s * groups : (s + 1) * groups, :]
+    each = KV_HEADS * groups
+    probs = [pr[s].astype(jnp.bfloat16) for s in range(seq_dev)]
+
+    def spread(k, carry):
+        o = peer_of(me, k, n)
+        for s in range(seq_dev):
+            pt[o, s * each : (s + 1) * each, :] = jnp.dot(
+                probs[s], tn[o, s * LEN : (s + 1) * LEN, :], preferred_element_type=jnp.float32
+            ).astype(jnp.bfloat16)
+        remote(pt.at[o], ptr.at[me], pt_sem.at[0, k], pt_sem.at[1, k], axis, o).start()
+        return carry
+
+    lax.fori_loop(1, n, spread, 0)
     for s in range(seq_dev):
-        probs = pr[s].reshape(each, LEN).astype(jnp.bfloat16)
-
-        def spread(o, carry, s=s, probs=probs):
-            one = jnp.dot(
-                probs, tn[o, s * LEN : (s + 1) * LEN, :], preferred_element_type=jnp.float32
-            ).astype(jnp.bfloat16)
-            pt[o, s * each : (s + 1) * each, :] = one
-            return carry
-
-        lax.fori_loop(0, n, spread, 0)
-    start_all(axis, n, lambda peer: pt.at[peer], ptr, pt_sem)
-    ptr[me] = pt[me]
+        ptr[me, s * each : (s + 1) * each, :] = jnp.dot(
+            probs[s], tn[me, s * LEN : (s + 1) * LEN, :], preferred_element_type=jnp.float32
+        ).astype(jnp.bfloat16)
     value_copy.wait()
     recv_all(axis, n, ptr, pt_sem)
     kpd = max(1, KV_HEADS // n)
+    spread_rows = seq_dev * each
+    proj[...] = jnp.dot(
+        ptr[...].reshape(n * spread_rows, rows), wv[...], preferred_element_type=jnp.float32
+    ).reshape(n, spread_rows, wv.shape[1])
 
     def project(src, carry):
-        full = jnp.dot(ptr[src], wv[...], preferred_element_type=jnp.float32)
         for o in range(n):
             for i in range(kpd):
                 k = o * heads_dev // groups + i
                 for s in range(seq_dev):
-                    part[o, i * seq_dev + s, src] = full[
-                        s * each + k * 8 : s * each + (k + 1) * 8, k * HEAD_DIM : (k + 1) * HEAD_DIM
+                    part[o, i, src, s * groups : (s + 1) * groups, :] = proj[
+                        src,
+                        s * each + k * groups : s * each + (k + 1) * groups,
+                        k * HEAD_DIM : (k + 1) * HEAD_DIM,
                     ]
         return carry
 
@@ -600,14 +611,14 @@
     k_cos, k_sin = table(jnp.arange(LEN, dtype=f32))
     kpd = max(1, KV_HEADS // n)
     q_rows = max(8, heads_dev * seq_dev)
-    each = KV_HEADS * 8
+    each = KV_HEADS * groups
     vmem = pl.BlockSpec(memory_space=pltpu.VMEM)
     anywhere = pl.BlockSpec(memory_space=pl.ANY)
     dma = pltpu.SemaphoreType.DMA
     mixed_pack, x_last, gains = pl.pallas_call(
         functools.partial(attend_kernel, n, seq_dev),
         out_shape=(
-            jax.ShapeDtypeStruct((kpd * seq_dev, n, 8, HEAD_DIM), f32),
+            jax.ShapeDtypeStruct((kpd, n, seq_dev * groups, HEAD_DIM), f32),
             jax.ShapeDtypeStruct((cands, width), f32),
             jax.ShapeDtypeStruct((n, 8, cols), f32),
         ),
@@ -626,12 +637,13 @@
             pltpu.VMEM((1, width), f32),
             pltpu.VMEM((n, q_rows, HEAD_DIM), f32),
             pltpu.VMEM((n, q_rows, HEAD_DIM), f32),
-            pltpu.VMEM((seq_dev, KV_HEADS, 8, HEAD_DIM), f32),
-            pltpu.VMEM((seq_dev, KV_HEADS, 8, LEN), f32),
+            pltpu.VMEM((KV_HEADS, seq_dev * groups, HEAD_DIM), f32),
+            pltpu.VMEM((seq_dev, heads, LEN), f32),
             pltpu.VMEM((n, seq_dev * each, cols), bf16),
             pltpu.VMEM((n, seq_dev * each, cols), bf16),
-            pltpu.VMEM((n, kpd * seq_dev, n, 8, HEAD_DIM), f32),
-            pltpu.VMEM((n, kpd * seq_dev, n, 8, HEAD_DIM), f32),
+            pltpu.VMEM((n, seq_dev * each, kvw), f32),
+            pltpu.VMEM((n, kpd, n, seq_dev * groups, HEAD_DIM), f32),
+            pltpu.VMEM((n, kpd, n, seq_dev * groups, HEAD_DIM), f32),
             dma((2, 2, n)),
             dma((2, 2, n)),
             dma((4,)),
@@ -658,8 +670,8 @@
         k_cos,
         k_sin,
     )
-    mixed = mixed_pack.reshape(kpd, seq_dev, n, 8, HEAD_DIM)[:, :, :, :groups]
-    mixed = mixed.transpose(2, 1, 0, 3, 4).reshape(cands, kpd * groups * HEAD_DIM).astype(bf16)
+    mixed = mixed_pack.reshape(kpd, n, seq_dev, groups, HEAD_DIM)
+    mixed = mixed.transpose(1, 2, 0, 3, 4).reshape(cands, kpd * groups * HEAD_DIM).astype(bf16)
     first = lax.rem(me * heads_dev, groups) if heads_dev < groups else 0
     mixed = lax.dynamic_slice_in_dim(mixed, first * HEAD_DIM, cols, 1)
     last_cols = lax.dynamic_slice_in_dim(x_last, me * cols, cols, 1)

time: 208 us -> 186 us (0.89)
  Pallas kernels: 189 us -> 166 us
    pallas_call x1, Pallas kernels: 146 us -> 126 us  [body(): pl.pallas_call(functools.partial(attend_kernel, n, seq_dev), out_shape=(j...]
where the time goes in v2:
time: 186 us; the launch traced here: 185 us
  Pallas kernels  166 us (89%)
  local copies, waits for them, and re-layouts  7.43 us (4%)
  other arithmetic  6.14 us (3%)
  between operations  3.33 us (2%)
    pallas_call x1, Pallas kernels, body(): pl.pallas_call(functools.partial(attend_kernel, n, seq_dev), out_shape=(j...  126 us
    pallas_call x1, Pallas kernels, body(): pl.pallas_call(functools.partial(feed_kernel, n, judges), out_shape=(jax....  40.5 us

profile of v2, /device:TPU:0, one launch (start us, length us, event | category | flops | bytes accessed | tf_op | source)
XLA Modules:
  0.0 184.9 jit_solution(9244837764101283046)
XLA Ops:
  0.6 0.0 copy-start
  0.6 0.7 dynamic_slice.15.own_len
  1.4 0.6 fusion.11
  4.6 0.9 constant_dynamic-slice_fusion.3
  5.6 1.0 fusion.2
  6.6 0.0 copy-start.4
  6.6 0.2 pad_maximum_fusion
  6.8 0.7 add_convert_fusion
  7.5 0.1 fusion.10
  7.6 0.1 pad_maximum_fusion.2
  7.7 0.1 pad.11.clone
  7.7 0.8 maximum_convert_fusion.gain_pack
  8.5 1.2 copy-done.1
  9.8 1.2 copy-done.2
  11.0 125.9 %shard_map.149 = (f32[1,8,8,128]{3,2,1,0:T(8,128)S(1)}, f32[16,4096]{1,0:T(8,128)S(1)}, f32[8,8,512]{2,1,0:T(8,128)S(1)}) custom-call(s32[2]{0:T(128)S(1)} %dynamic_slice.15.own_len, bf16[1024,4096]{1,0:T(8,128)(2,1)} %bitcast.25, bf16[4096,512]{1,0:T(8,128)(2,1)} %bitcast.26, bf16[512,1024]{1,0:T(8,128)(2,1)S(1)} %bitcast.20, ...), custom_call_target="tpu_custom_call" | custom-call | tf_op jit(solution)/shard_map/pallas_call | solution.py:618
  136.9 0.0 copy-start.3
  136.9 0.6 copy-done.3
  137.5 0.6 constant_dynamic-slice_fusion.1.last_cols
  138.1 0.6 convert_element_type.20.mixed
  138.8 0.0 copy-done
  138.8 0.6 constant_dynamic-slice_fusion.reward
  139.3 0.6 convert_element_type.21.gain_final
  139.9 40.5 %shard_map.150 = (f32[16,512]{1,0:T(8,128)}, f32[16,128]{1,0:T(8,128)}) custom-call(bf16[16,512]{1,0:T(8,128)(2,1)} %convert_element_type.20.mixed, f32[16,512]{1,0:T(8,128)} %constant_dynamic-slice_fusion.1.last_cols, f32[8,8,512]{2,1,0:T(8,128)} %copy-done.3, f32[1,512]{1,0:T(1,128)} %convert_element_type.21.gain_final, ...), custom_call_target="tpu_custom_call" | custom-call | tf_op jit(solution)/shard_map/pallas_call | solution.py:680
  180.5 0.9 fusion.8
  181.3 0.0 copy-done.5
  181.3 0.2 fusion.6
  181.5 0.2 fusion.7
  181.7 0.1 copy.21
  181.8 0.1 copy.20
  181.9 0.9 multiply_reduce_fusion
  182.8 1.6 fusion.3
  184.4 0.5 div.15
  (10 shorter events, 0.1 us)
Async XLA Ops:
  0.6 138.1 %copy-start = (f32[1,4096]{1,0:T(1,128)S(1)}, f32[1,4096]{1,0:T(1,128)}, u32[]{:S(2)}) copy-start(f32[1,4096]{1,0:T(1,128)} %param.27) | copy-start | bytes 49156
  6.6 132.8 %copy-start.4 = (bf16[1,512]{1,0:T(2,128)(2,1)S(1)}, bf16[1,512]{1,0:T(2,128)(2,1)}, u32[]{:S(2)}) copy-start(bf16[1,512]{1,0:T(2,128)(2,1)} %param.26) | copy-start | bytes 3076
  8.5 1.2 copy-start.1
  9.8 1.2 copy-start.2
  136.9 0.6 copy-start.3
  139.9 41.4 %copy-start.5 = (s32[16]{0:T(128)S(1)}, s32[16]{0:T(128)}, u32[]{:S(2)}) copy-start(s32[16]{0:T(128)} %param.16) | copy-start | bytes 196
